TPU v7x, 32 devices: a whole 2x2x4 slice. The times are simulated.
32 devices in a mesh: ctx: 8 (over z, core), tp: 4 (over y, x).
Axes of the slice: x: 2, y: 2, z: 4, core: 2. Of those that a mesh axis runs over, the one named last changes fastest.
Arguments:
- query_latent: bfloat16 [4096, 64, 512], P('ctx', 'tp'), may hold values from -24 to 24
- query_rope: bfloat16 [4096, 4096], P('ctx', 'tp'), may hold values from -24 to 24
- key_latent: bfloat16 [4096, 512], P('ctx'), may hold values from -6 to 6
- key_rope: bfloat16 [2048, 128], P('ctx'), may hold values from -6 to 6
- block_ids: int32 [16], replicated, may hold values from 0 to 15, as said below
- value_up: bfloat16 [64, 512, 128], P('tp'), may hold values from -0.5 to 0.5
- out_weight: bfloat16 [8192, 7168], P('tp'), may hold values from -0.0625 to 0.0625
- residual: bfloat16 [4096, 7168], P(('ctx', 'tp')), may hold values from -18 to 18
- norm_gain: float32 [7168], replicated, may hold values from 0.1 to 1.9
- gate_weight: bfloat16 [7168, 2048], P('ctx', 'tp'), may hold values from -0.0625 to 0.0625
- up_weight: bfloat16 [7168, 2048], P('ctx', 'tp'), may hold values from -0.0625 to 0.0625
- down_weight: bfloat16 [7168, 2048], P('ctx', 'tp'), may hold values from -0.125 to 0.125
Outputs:
- layer_out: bfloat16 [4096, 7168], P(('ctx', 'tp'))
Inputs may be any that keep to these rules, and one draw needn't show every extreme that they name: `block_ids`: index c of ctx stores blocks 2c and 2c + 1; their two entries sum to 15, and every value appears once.
All inputs are finite; a program needn't handle non-finite values.
Results may differ from a plain program's by a relative error of at most 0.018.
Values may be sent and summed in bfloat16 or wider, within the bound.
A program may use at most 192 MiB of HBM per device.

v0:
```python
import jax
import jax.numpy as jnp
from jax import lax
from jax.sharding import PartitionSpec as P


def from_behind(x, axis, by):
    length = lax.axis_size(axis)
    return lax.ppermute(x, axis, [(i, (i + by) % length) for i in range(length)])


def rms_norm(activation, gain_vector):
    mean_square = jnp.mean(activation * activation, axis=-1, keepdims=True)
    return (activation * lax.rsqrt(mean_square + 1e-06) * gain_vector).astype(jnp.bfloat16)


def local(
    query_latent,
    query_rope,
    key_latent,
    key_rope,
    block_ids,
    value_up,
    out_weight,
    residual,
    norm_gain,
    gate_weight,
    up_weight,
    down_weight,
):
    seq_rows = key_latent.shape[0]
    half_len = seq_rows // 2
    head_count = query_latent.shape[1]
    rope_dim = key_rope.shape[1] // 2
    head_dim = value_up.shape[2]
    ctx_count = lax.axis_size("ctx")
    tp_count = lax.axis_size("tp")
    score_scale = (head_dim + rope_dim) ** (-0.5)
    recv_latent, recv_rope = from_behind((key_latent, key_rope), "ctx", 1)
    keys_lat = jnp.concatenate([key_latent, recv_latent], axis=0)
    keys_rot = jnp.concatenate(
        [key_rope.reshape(seq_rows, rope_dim), recv_rope.reshape(seq_rows, rope_dim)], axis=0
    )
    current = lax.axis_index("ctx")
    previous = (current + ctx_count - 1) % ctx_count
    own_ids = lax.dynamic_slice_in_dim(block_ids, current * 2, 2, 0)
    prev_ids = lax.dynamic_slice_in_dim(block_ids, previous * 2, 2, 0)
    row_index = jnp.arange(seq_rows, dtype=jnp.int32)
    first_half = row_index < half_len
    offset = row_index % half_len
    query_pos = jnp.where(first_half, own_ids[0], own_ids[1]) * half_len + offset
    key_pos = jnp.concatenate(
        [query_pos, jnp.where(first_half, prev_ids[0], prev_ids[1]) * half_len + offset], axis=0
    )
    rope_queries = query_rope.reshape(seq_rows, head_count, rope_dim)
    block_rows = min(seq_rows, 512)

    def attend(block_index):
        scores = jnp.einsum(
            "shl,kl->hsk", query_latent, keys_lat, preferred_element_type=jnp.float32
        )
        scores = scores + jnp.einsum(
            "shr,kr->hsk", rope_queries, keys_rot, preferred_element_type=jnp.float32
        )
        scores = scores * score_scale
        visible = key_pos[None, :] <= query_pos[:, None]
        scores = jnp.where(visible[None], scores, -jnp.inf)
        highest = jnp.max(scores, axis=-1, keepdims=True)
        exponent = jnp.exp(scores - highest)
        weights = (exponent / jnp.sum(exponent, axis=-1, keepdims=True)).astype(jnp.bfloat16)
        blended = jnp.einsum(
            "hsk,kl->shl", weights, keys_lat, preferred_element_type=jnp.float32
        ).astype(jnp.bfloat16)
        values = jnp.einsum(
            "shl,hlv->shv", blended, value_up, preferred_element_type=jnp.float32
        ).astype(jnp.bfloat16)
        return values.reshape(block_rows, head_count * head_dim)

    head_out = lax.map(attend, jnp.arange(seq_rows // block_rows, dtype=jnp.int32)).reshape(
        seq_rows, head_count * head_dim
    )
    share_rows = seq_rows // tp_count
    tp_index = lax.axis_index("tp")
    partial_attn = jnp.dot(head_out, out_weight, preferred_element_type=jnp.float32)
    attn_total = lax.psum(partial_attn.astype(jnp.bfloat16), "tp").astype(jnp.float32)
    all_residual = lax.all_gather(residual, "tp", axis=0, tiled=True)
    hidden_state = all_residual.astype(jnp.float32) + attn_total
    normed_all = rms_norm(hidden_state, norm_gain)
    own_state = lax.dynamic_slice_in_dim(hidden_state, tp_index * share_rows, share_rows, 0)
    gate_full, up_full, down_full = (
        lax.all_gather(gate_weight, "ctx", axis=0, tiled=True),
        lax.all_gather(up_weight, "ctx", axis=0, tiled=True),
        lax.all_gather(down_weight, "ctx", axis=0, tiled=True),
    )
    gate_proj = jnp.dot(normed_all, gate_full, preferred_element_type=jnp.float32)
    up_proj = jnp.dot(normed_all, up_full, preferred_element_type=jnp.float32)
    hidden_units = (jax.nn.silu(gate_proj) * up_proj).astype(jnp.bfloat16)
    shared_part = lax.psum_scatter(
        lax.dot_general(
            hidden_units, down_full, (((1,), (1,)), ((), ())), preferred_element_type=jnp.float32
        ).astype(jnp.bfloat16),
        "tp",
        scatter_dimension=0,
        tiled=True,
    ).astype(jnp.float32)
    return (own_state + shared_part).astype(jnp.bfloat16)


def solution(mesh):
    placed = (
        P("ctx", "tp", None),
        P("ctx", "tp"),
        P("ctx", None),
        P("ctx", None),
        P(),
        P("tp", None, None),
        P("tp", None),
        P(("ctx", "tp"), None),
        P(),
        P("ctx", "tp"),
        P("ctx", "tp"),
        P("ctx", "tp"),
    )
    return jax.shard_map(
        local, mesh=mesh, in_specs=placed, out_specs=P(("ctx", "tp"), None), check_vma=False
    )
```

profile of v0, /device:TPU:0, one launch (start us, length us, event | category | flops | bytes accessed | tf_op | source)
XLA Modules:
  0.0 672.1 jit_solution(7638917272089841626)
XLA Ops:
  6.5 0.0 copy-start
  6.5 0.0 all-reduce.2.cloned.1.call-start
  6.5 0.5 collective-permute-start
  7.0 2.7 collective-permute-start.1
  9.7 0.8 fusion.35
  10.5 0.6 fusion.34
  11.1 1.2 fusion.22
  12.3 1.3 multiply_add_fusion
  13.6 1.2 broadcast_compare_fusion
  14.8 0.9 reshape.69
  15.7 1.5 copy.19
  17.2 0.1 copy.17
  17.3 1.5 collective-permute-done.1
  18.8 0.1 reshape.70
  18.9 0.1 copy.18
  19.0 0.0 collective-permute-done
  19.0 18.1 %fusion.3 = f32[1024,512,16]{1,0,2:T(8,128)} fusion(bf16[512,16,512]{2,1,0:T(8,128)(2,1)} %param.12, bf16[512,512]{1,0:T(8,128)(2,1)} %collective-permute-done, bf16[512,512]{1,0:T(8,128)(2,1)} %param.14), kind=kOutput, calls=%fused_computation.11 | convolution fusion | flops 8592031744 | bytes 42991616 | tf_op jit(solution)/shard_map/while/body/eval_jaxpr/shl,kl->hsk/dot_general | solution.py:59
  37.1 24.3 %fusion.37 = (f32[16,512]{1,0:T(8,128)S(1)}, f32[16,512,1024]{1,2,0:T(8,128)}) fusion(f32[1024,512,16]{1,0,2:T(8,128)} %fusion.3, pred[512,1024]{0,1:T(8,128)(4,1)} %broadcast_compare_fusion, bf16[512,16,64]{0,2,1:T(8,128)(2,1)S(1)} %bitcast.36, bf16[512,64]{0,1:T(8,128)(2,1)S(1)} %copy.18, bf16[512,64]{0,1:T(8,128)(2,1)S(1)} %copy.17), kind=kOutput, calls=%fused_computation.51 | convolution fusion | flops 1115948032 | bytes 68845568 | tf_op jit(solution)/shard_map/while/body/eval_jaxpr/sub | solution.py:69
  61.3 0.0 copy-done
  61.3 17.5 %fusion.9 = bf16[16,512,128]{1,2,0:T(8,128)(2,1)} fusion(bf16[16,512,128]{2,1,0:T(8,128)(2,1)S(1)} %copy-done, f32[16,512,1024]{1,2,0:T(8,128)} %get-tuple-element.41, f32[16,512]{1,0:T(8,128)S(1)} %get-tuple-element.40, bf16[512,512]{1,0:T(8,128)(2,1)} %collective-permute-done, bf16[512,512]{1,0:T(8,128)(2,1)} %param.14), kind=kOutput, calls=%fused_computation.17 | convolution fusion | flops 9687793664 | bytes 38830080 | tf_op jit(solution)/shard_map/while/body/eval_jaxpr/shl,hlv->shv/dot_general | solution.py:74
  78.9 23.3 %convolution_convert_fusion.1 = bf16[512,7168]{1,0:T(8,128)(2,1)} fusion(bf16[512,2048]{0,1:T(8,128)(2,1)} %bitcast.37, bf16[2048,7168]{1,0:T(8,128)(2,1)} %param.18), kind=kOutput, calls=%fused_computation.10 | convolution fusion | flops 15036055552 | bytes 38797312 | tf_op jit(solution)/shard_map/dot_general | solution.py:84
  102.2 0.0 all-reduce.2.cloned.1.call-update
  102.2 0.0 all-gather.5.cloned.1.call-start
  102.3 0.7 all-gather.5.cloned.1.call-update
  103.0 0.0 all-gather.7.cloned.1.call-start
  103.0 0.7 all-gather.7.cloned.1.call-update
  103.7 0.0 all-gather.11.cloned.1.call-start
  103.7 0.5 all-gather.11.cloned.1.call-update
  104.3 0.0 all-gather.9.cloned.1.call-start
  104.3 0.5 all-gather.9.cloned.1.call-update
  104.9 0.0 copy-start.2
  104.9 0.0 reduce-scatter.2.cloned.1.call-start
  104.9 153.2 %all-reduce.2.cloned.1.call-done = bf16[512,7168]{1,0:T(8,128)(2,1)} async-done(((bf16[512,7168]{1,0:T(8,128)(2,1)}), bf16[512,7168]{1,0:T(8,128)(2,1)}) %all-reduce.2.cloned.1.call-update) | async-done | bytes 7340048 | tf_op jit(solution)/shard_map/psum | solution.py:85
  258.1 80.8 %all-gather.5.cloned.1.call-done = bf16[512,7168]{1,0:T(8,128)(2,1)} async-done(((bf16[128,7168]{1,0:T(8,128)(2,1)}), bf16[512,7168]{1,0:T(8,128)(2,1)}) %all-gather.5.cloned.1.call-update) | async-done | bytes 7340048 | tf_op jit(solution)/shard_map/all_gather | solution.py:86
  338.9 13.5 %convert_add_fusion = (f32[512,7168]{1,0:T(8,128)}, f32[512]{0:T(512)S(1)}) fusion(bf16[512,7168]{1,0:T(8,128)(2,1)} %all-reduce.2.cloned.1.call-done, bf16[512,7168]{1,0:T(8,128)(2,1)} %all-gather.5.cloned.1.call-done), kind=kLoop, calls=%fused_computation.7 | loop fusion | flops 18349568 | bytes 29362176 | tf_op jit(solution)/shard_map/add | solution.py:87
  352.4 61.6 %all-gather.7.cloned.1.call-done = bf16[7168,512]{1,0:T(8,128)(2,1)} async-done(((bf16[896,512]{1,0:T(8,128)(2,1)}), bf16[7168,512]{1,0:T(8,128)(2,1)}) %all-gather.7.cloned.1.call-update) | async-done | bytes 7340048 | tf_op jit(solution)/shard_map/all_gather | solution.py:91
  413.9 0.0 copy-done.2
  413.9 9.7 %fusion.33 = f32[512,512]{1,0:T(8,128)S(1)} fusion(bf16[7168,512]{1,0:T(8,128)(2,1)} %all-gather.7.cloned.1.call-done, f32[7168]{0:T(1024)S(1)} %copy-done.2, f32[512]{0:T(512)S(1)} %add_rsqrt_fusion, bf16[512,7168]{1,0:T(8,128)(2,1)} %all-reduce.2.cloned.1.call-done, bf16[512,7168]{1,0:T(8,128)(2,1)} %all-gather.5.cloned.1.call-done), kind=kOutput, calls=%fused_computation.47 | convolution fusion | flops 3780116480 | bytes 23099392 | tf_op jit(solution)/shard_map/dot_general | solution.py:95
  423.7 63.8 %all-gather.11.cloned.1.call-done = bf16[7168,512]{1,0:T(8,128)(2,1)} async-done(((bf16[896,512]{1,0:T(8,128)(2,1)}), bf16[7168,512]{1,0:T(8,128)(2,1)}) %all-gather.11.cloned.1.call-update) | async-done | bytes 7340048 | tf_op jit(solution)/shard_map/all_gather | solution.py:93
  487.5 73.5 %all-gather.9.cloned.1.call-done = bf16[7168,512]{1,0:T(8,128)(2,1)} async-done(((bf16[896,512]{1,0:T(8,128)(2,1)}), bf16[7168,512]{1,0:T(8,128)(2,1)}) %all-gather.9.cloned.1.call-update) | async-done | bytes 7340048 | tf_op jit(solution)/shard_map/all_gather | solution.py:92
  561.0 22.3 %convolution_convert_fusion = bf16[512,7168]{1,0:T(8,128)(2,1)} fusion(bf16[7168,512]{1,0:T(8,128)(2,1)} %all-gather.11.cloned.1.call-done, bf16[7168,512]{1,0:T(8,128)(2,1)} %all-gather.9.cloned.1.call-done, f32[512,512]{1,0:T(8,128)S(1)} %fusion.33, f32[7168]{0:T(1024)S(1)} %copy-done.2, f32[512]{0:T(512)S(1)} %add_rsqrt_fusion, ...), kind=kOutput, calls=%fused_computation.9 | convolution fusion | flops 7543455744 | bytes 37779456 | tf_op jit(solution)/shard_map/dot_general | solution.py:99
  583.3 0.0 copy-start.1
  583.3 0.0 reduce-scatter.2.cloned.1.call-update
  583.3 77.7 %reduce-scatter.2.cloned.1.call-done = bf16[128,7168]{1,0:T(8,128)(2,1)} async-done(((bf16[512,7168]{1,0:T(8,128)(2,1)}), bf16[128,7168]{1,0:T(8,128)(2,1)}) %reduce-scatter.2.cloned.1.call-update) | async-done | bytes 1835024 | tf_op jit(solution)/shard_map/reduce_scatter | solution.py:98
  661.1 4.2 add_convert_fusion
  665.2 0.0 copy-done.1
  (2 shorter events, 0.0 us)
Async XLA Ops:
  6.5 54.8 %copy-start = (bf16[16,512,128]{2,1,0:T(8,128)(2,1)S(1)}, bf16[16,512,128]{2,1,0:T(8,128)(2,1)}, u32[]{:S(2)}) copy-start(bf16[16,512,128]{2,1,0:T(8,128)(2,1)} %param.17) | copy-start | bytes 6291460
  6.5 251.6 %all-reduce.2.cloned.1.call-start = ((), (), s32[]{:S(2)}) async-start(), calls=%async_computation.2 | async-start | bytes 14680064 | tf_op jit(solution)/shard_map/psum | solution.py:85
  6.5 12.5 %collective-permute-start = (bf16[512,512]{1,0:T(8,128)(2,1)}, bf16[512,512]{1,0:T(8,128)(2,1)}, u32[]{:S(2)}, u32[]{:S(2)}) collective-permute-start(bf16[512,512]{1,0:T(8,128)(2,1)} %param.14), channel_id=1, source_target_pairs={{0,4},{4,8},{8,12},{12,16},{16,20},{20,24},{24,28},{28,0},{1,5},{5... | collective-permute-start | bytes 1572872 | tf_op jit(solution)/shard_map/ppermute | solution.py:9
  7.0 11.8 %collective-permute-start.1 = (bf16[256,128]{1,0:T(8,128)(2,1)}, bf16[256,128]{1,0:T(8,128)(2,1)S(1)}, u32[]{:S(2)}, u32[]{:S(2)}) collective-permute-start(bf16[256,128]{1,0:T(8,128)(2,1)} %param.15), channel_id=1, source_target_pairs={{0,4},{4,8},{8,12},{12,16},{16,20},{20,24},{24,28},{28,0},{1,5},{5... | collective-permute-start | bytes 196616 | tf_op jit(solution)/shard_map/ppermute | solution.py:9
  102.2 236.6 %all-gather.5.cloned.1.call-start = ((), (), s32[]{:S(2)}) async-start(), calls=%async_computation.1 | async-start | bytes 9175040 | tf_op jit(solution)/shard_map/all_gather | solution.py:86
  103.0 311.0 %all-gather.7.cloned.1.call-start = ((), (), s32[]{:S(2)}) async-start(), calls=%async_computation.3 | async-start | bytes 8257536 | tf_op jit(solution)/shard_map/all_gather | solution.py:91
  103.7 383.8 %all-gather.11.cloned.1.call-start = ((), (), s32[]{:S(2)}) async-start(), calls=%async_computation.5 | async-start | bytes 8257536 | tf_op jit(solution)/shard_map/all_gather | solution.py:93
  104.3 456.7 %all-gather.9.cloned.1.call-start = ((), (), s32[]{:S(2)}) async-start(), calls=%async_computation.4 | async-start | bytes 8257536 | tf_op jit(solution)/shard_map/all_gather | solution.py:92
  104.9 309.1 %copy-start.2 = (f32[7168]{0:T(1024)S(1)}, f32[7168]{0:T(1024)}, u32[]{:S(2)}) copy-start(f32[7168]{0:T(1024)} %param.20) | copy-start | bytes 86020
  104.9 556.2 %reduce-scatter.2.cloned.1.call-start = ((), (), s32[]{:S(2)}) async-start(), calls=%async_computation.6 | async-start | bytes 9175040 | tf_op jit(solution)/shard_map/reduce_scatter | solution.py:98
  583.3 81.9 %copy-start.1 = (bf16[16,512,128]{2,1,0:T(8,128)(2,1)S(1)}, bf16[16,512,128]{2,1,0:T(8,128)(2,1)}, u32[]{:S(2)}) copy-start(bf16[16,512,128]{2,1,0:T(8,128)(2,1)} %param.17) | copy-start | bytes 6291460
Sparse Core Ops, SparseCore 0:
  102.3 155.7 all-reduce.1
  259.9 78.8 all-gather.4
  340.5 73.3 all-gather.6
  415.4 71.9 all-gather.10
  489.0 71.9 all-gather.8
  583.5 77.5 reduce-scatter.1
where the time goes:
time: 672 us
  waiting for transfers between devices  515 us (77%)
  matrix products  115 us (17%)
  other arithmetic  21.3 us (3%)
  between operations  13.6 us (2%)
    psum x1, waiting for transfers between devices, local(): lax.psum(partial_attn.astype(jnp.bfloat16), 'tp').astype(jnp.float32)  153 us
    all_gather x1, waiting for transfers between devices, local(): all_residual = lax.all_gather(residual, 'tp', axis=0, tiled=True)  80.8 us
    reduce_scatter x1, waiting for transfers between devices, local(): lax.psum_scatter(lax.dot_general(hidden_units, down_full, (((1,), (1,)),...  77.7 us
    all_gather x1, waiting for transfers between devices, local(): lax.all_gather(up_weight, 'ctx', axis=0, tiled=True)  73.5 us
    all_gather x1, waiting for transfers between devices, local(): lax.all_gather(down_weight, 'ctx', axis=0, tiled=True)  63.8 us
    all_gather x1, waiting for transfers between devices, local(): lax.all_gather(gate_weight, 'ctx', axis=0, tiled=True)  61.6 us
    sub x1, matrix products, attend(): exponent = jnp.exp(scores - highest)  24.3 us
    dot_general x1, matrix products, local(): jnp.dot(head_out, out_weight, preferred_element_type=jnp.float32)  23.3 us
  transfers between devices with their start and end apart: 8, of which 7 were waited for; matrix products, arithmetic and copies ran while one was open for 5% of the time, Pallas kernels for 0%

commit v1 on v0

--- a/solution.py
+++ b/solution.py
@@ -2,6 +2,17 @@
 import jax.numpy as jnp
 from jax import lax
 from jax.sharding import PartitionSpec as P
+
+
+def pass_along(x, mesh_axis, dim):
+    peers = lax.axis_size(mesh_axis)
+    hops = [(i, (i + 1) % peers) for i in range(peers)]
+    parts = [x]
+    for far in range(1, peers):
+        parts = [lax.ppermute(parts[0], mesh_axis, hops), *parts]
+    result = jnp.concatenate(parts, axis=dim)
+    shift = (lax.axis_index(mesh_axis) + 1) * parts[-1].shape[dim]
+    return jnp.roll(result, shift, axis=dim)
 
 
 def from_behind(x, axis, by):
@@ -83,7 +94,7 @@
     tp_index = lax.axis_index("tp")
     partial_attn = jnp.dot(head_out, out_weight, preferred_element_type=jnp.float32)
     attn_total = lax.psum(partial_attn.astype(jnp.bfloat16), "tp").astype(jnp.float32)
-    all_residual = lax.all_gather(residual, "tp", axis=0, tiled=True)
+    all_residual = pass_along(residual, "tp", 0)
     hidden_state = all_residual.astype(jnp.float32) + attn_total
     normed_all = rms_norm(hidden_state, norm_gain)
     own_state = lax.dynamic_slice_in_dim(hidden_state, tp_index * share_rows, share_rows, 0)

time: 672 us -> 480 us (0.71)
  waiting for transfers between devices: 515 us -> 294 us
  local copies, waits for them, and re-layouts: 4.16 us -> 24.6 us
    ppermute x0 -> x3, waiting for transfers between devices: none -> 203 us  [pass_along(): parts = [lax.ppermute(parts[0], mesh_axis, hops), *parts]]
    psum x1, waiting for transfers between devices: 153 us -> 8.62 us  [local(): lax.psum(partial_attn.astype(jnp.bfloat16), 'tp').astype(jnp.float32)]
    all_gather x1 -> x0, waiting for transfers between devices: 80.8 us -> none  [local(): all_residual = lax.all_gather(residual, 'tp', axis=0, tiled=True)]
    all_gather x1, waiting for transfers between devices: 73.5 us -> 0.03 us  [local(): lax.all_gather(up_weight, 'ctx', axis=0, tiled=True)]
    all_gather x1, waiting for transfers between devices: 63.8 us -> 0.02 us  [local(): lax.all_gather(down_weight, 'ctx', axis=0, tiled=True)]
    all_gather x1, waiting for transfers between devices: 61.6 us -> 0.01 us  [local(): lax.all_gather(gate_weight, 'ctx', axis=0, tiled=True)]
    unnamed x7 -> x16, local copies, waits for them, and re-layouts: 1.51 us -> 20.5 us
    add x1 -> x0, other arithmetic: 13.5 us -> none  [local(): hidden_state = all_residual.astype(jnp.float32) + attn_total]
  transfers between devices with their start and end apart: 8 -> 10, of which waited for: 7 -> 6; matrix products, arithmetic and copies ran while one was open for 5% -> 11% of each run, Pallas kernels for 0% -> 0%
where the time goes in v1:
time: 480 us
  waiting for transfers between devices  294 us (61%)
  matrix products  116 us (24%)
  local copies, waits for them, and re-layouts  24.6 us (5%)
  other arithmetic  20.6 us (4%)
  between operations  15.2 us (3%)
  starting transfers between devices  9.76 us (2%)
    ppermute x3, waiting for transfers between devices, pass_along(): parts = [lax.ppermute(parts[0], mesh_axis, hops), *parts]  203 us
    reduce_scatter x1, waiting for transfers between devices, local(): lax.psum_scatter(lax.dot_general(hidden_units, down_full, (((1,), (1,)),...  80.3 us
    sub x1, matrix products, attend(): exponent = jnp.exp(scores - highest)  24.3 us
    dot_general x1, matrix products, local(): jnp.dot(head_out, out_weight, preferred_element_type=jnp.float32)  23.4 us
    dot_general x1, matrix products, local(): lax.dot_general(hidden_units, down_full, (((1,), (1,)), ((), ())), prefer...  22.5 us
    unnamed x16, local copies, waits for them, and re-layouts  20.5 us
    dot_general x1, matrix products, attend(): jnp.einsum('shl,kl->hsk', query_latent, keys_lat, preferred_element_type=...  18.1 us
    dot_general x1, matrix products, attend(): jnp.einsum('shl,hlv->shv', blended, value_up, preferred_element_type=jnp....  17.5 us
  transfers between devices with their start and end apart: 10, of which 6 were waited for; matrix products, arithmetic and copies ran while one was open for 11% of the time, Pallas kernels for 0%

profile of v1, /device:TPU:0, one launch (start us, length us, event | category | flops | bytes accessed | tf_op | source)
XLA Modules:
  0.0 480.0 jit_solution(12273457680901332404)
XLA Ops:
  7.4 0.0 copy-start
  7.4 0.0 all-reduce.2.cloned.1.call-start
  7.4 0.5 collective-permute-start.3
  7.8 2.7 collective-permute-start.4
  10.5 0.8 fusion.35
  11.3 0.6 fusion.34
  11.9 1.3 fusion.22
  13.2 1.2 multiply_add_fusion
  14.4 1.2 broadcast_compare_fusion
  15.6 0.9 reshape.69
  16.5 1.5 copy.19
  18.0 0.1 copy.17
  18.1 1.5 collective-permute-done.4
  19.6 0.1 reshape.70
  19.7 0.1 copy.18
  19.9 0.0 collective-permute-done.3
  19.9 18.1 %fusion.3 = f32[1024,512,16]{1,0,2:T(8,128)} fusion(bf16[512,16,512]{2,1,0:T(8,128)(2,1)} %param.12, bf16[512,512]{1,0:T(8,128)(2,1)} %collective-permute-done.3, bf16[512,512]{1,0:T(8,128)(2,1)} %param.14), kind=kOutput, calls=%fused_computation.11 | convolution fusion | flops 8592031744 | bytes 42991616 | tf_op jit(solution)/shard_map/while/body/eval_jaxpr/shl,kl->hsk/dot_general | solution.py:70
  37.9 24.3 %fusion.37 = (f32[16,512]{1,0:T(8,128)S(1)}, f32[16,512,1024]{1,2,0:T(8,128)}) fusion(f32[1024,512,16]{1,0,2:T(8,128)} %fusion.3, pred[512,1024]{0,1:T(8,128)(4,1)} %broadcast_compare_fusion, bf16[512,16,64]{0,2,1:T(8,128)(2,1)S(1)} %bitcast.36, bf16[512,64]{0,1:T(8,128)(2,1)S(1)} %copy.18, bf16[512,64]{0,1:T(8,128)(2,1)S(1)} %copy.17), kind=kOutput, calls=%fused_computation.59 | convolution fusion | flops 1115948032 | bytes 68845568 | tf_op jit(solution)/shard_map/while/body/eval_jaxpr/sub | solution.py:80
  62.2 0.0 copy-done
  62.2 17.5 %fusion.9 = bf16[16,512,128]{1,2,0:T(8,128)(2,1)} fusion(bf16[16,512,128]{2,1,0:T(8,128)(2,1)S(1)} %copy-done, f32[16,512,1024]{1,2,0:T(8,128)} %get-tuple-element.41, f32[16,512]{1,0:T(8,128)S(1)} %get-tuple-element.40, bf16[512,512]{1,0:T(8,128)(2,1)} %collective-permute-done.3, bf16[512,512]{1,0:T(8,128)(2,1)} %param.14), kind=kOutput, calls=%fused_computation.17 | convolution fusion | flops 9687793664 | bytes 38830080 | tf_op jit(solution)/shard_map/while/body/eval_jaxpr/shl,hlv->shv/dot_general | solution.py:85
  79.7 0.0 copy-start.2
  79.7 23.4 %convolution_convert_fusion.1 = bf16[512,7168]{1,0:T(8,128)(2,1)} fusion(bf16[512,2048]{0,1:T(8,128)(2,1)} %bitcast.37, bf16[2048,7168]{1,0:T(8,128)(2,1)} %param.18), kind=kOutput, calls=%fused_computation.10 | convolution fusion | flops 15036055552 | bytes 38797312 | tf_op jit(solution)/shard_map/dot_general | solution.py:95
  103.2 0.0 all-reduce.2.cloned.1.call-update
  103.2 0.0 all-gather.4.cloned.1.call-start
  103.2 0.5 all-gather.4.cloned.1.call-update
  103.8 0.0 all-gather.6.cloned.1.call-start
  103.8 0.5 all-gather.6.cloned.1.call-update
  104.4 0.0 all-gather.8.cloned.1.call-start
  104.4 0.0 copy-done.2
  104.4 2.1 collective-permute-start
  106.5 0.0 all-gather.8.cloned.1.call-update
  106.5 0.0 reduce-scatter.2.cloned.1.call-start
  106.6 77.9 %collective-permute-done = bf16[128,7168]{1,0:T(8,128)(2,1)} collective-permute-done((bf16[128,7168]{1,0:T(8,128)(2,1)S(1)}, bf16[128,7168]{1,0:T(8,128)(2,1)}, u32[]{:S(2)}, u32[]{:S(2)}) %collective-permute-start) | collective-permute-done | bytes 1835040 | tf_op jit(solution)/shard_map/ppermute | solution.py:12
  184.4 2.6 collective-permute-start.1
  187.0 57.5 %collective-permute-done.1 = bf16[128,7168]{1,0:T(8,128)(2,1)} collective-permute-done((bf16[128,7168]{1,0:T(8,128)(2,1)}, bf16[128,7168]{1,0:T(8,128)(2,1)}, u32[]{:S(2)}, u32[]{:S(2)}) %collective-permute-start.1) | collective-permute-done | bytes 1835040 | tf_op jit(solution)/shard_map/ppermute | solution.py:12
  244.6 1.8 collective-permute-start.2
  246.4 67.4 %collective-permute-done.2 = bf16[128,7168]{1,0:T(8,128)(2,1)} collective-permute-done((bf16[128,7168]{1,0:T(8,128)(2,1)}, bf16[128,7168]{1,0:T(8,128)(2,1)}, u32[]{:S(2)}, u32[]{:S(2)}) %collective-permute-start.2) | collective-permute-done | bytes 1835040 | tf_op jit(solution)/shard_map/ppermute | solution.py:12
  313.8 3.0 constant_dynamic-update-slice_fusion.7
  316.8 2.9 constant_dynamic-update-slice_fusion.6
  319.6 3.0 constant_dynamic-update-slice_fusion.5
  322.6 1.4 constant_dynamic-update-slice_fusion.4
  324.0 3.0 constant_dynamic-update-slice_fusion.3
  327.0 2.9 constant_dynamic-update-slice_fusion.2
  330.0 2.9 constant_dynamic-update-slice_fusion.1
  332.8 1.4 constant_dynamic-update-slice_fusion
  334.2 0.0 copy-start.3
  334.2 8.6 %all-reduce.2.cloned.1.call-done = bf16[512,7168]{1,0:T(8,128)(2,1)} async-done(((bf16[512,7168]{1,0:T(8,128)(2,1)}), bf16[512,7168]{1,0:T(8,128)(2,1)}) %all-reduce.2.cloned.1.call-update) | async-done | bytes 7340048 | tf_op jit(solution)/shard_map/psum | solution.py:96
  342.8 12.8 %multiply_reduce_fusion = (f32[512]{0:T(512)S(1)}, f32[512,7168]{1,0:T(8,128)}) fusion(bf16[512,7168]{1,0:T(8,128)(2,1)} %all-reduce.2.cloned.1.call-done, bf16[1024,7168]{1,0:T(8,128)(2,1)} %constant_dynamic-update-slice_fusion, s32[]{:T(128)S(6)} %select_n.57), kind=kLoop, calls=%fused_computation.6 | loop fusion | flops 18349568 | bytes 29362180 | tf_op jit(solution)/shard_map/reduce_sum | solution.py:24
  355.6 0.0 all-gather.4.cloned.1.call-done
  355.6 0.0 copy-done.3
  355.6 9.7 %fusion.33 = f32[512,512]{1,0:T(8,128)S(1)} fusion(bf16[7168,512]{1,0:T(8,128)(2,1)} %all-gather.4.cloned.1.call-done, f32[512,7168]{1,0:T(8,128)} %get-tuple-element.22, f32[7168]{0:T(1024)S(1)} %copy-done.3, f32[512]{0:T(512)S(1)} %add_rsqrt_fusion), kind=kOutput, calls=%fused_computation.55 | convolution fusion | flops 3769106432 | bytes 23099392 | tf_op jit(solution)/shard_map/dot_general | solution.py:106
  365.3 0.0 all-gather.6.cloned.1.call-done
  365.3 0.0 all-gather.8.cloned.1.call-done
  365.4 0.0 copy-start.1
  365.4 22.5 %convolution_convert_fusion = bf16[512,7168]{1,0:T(8,128)(2,1)} fusion(bf16[7168,512]{1,0:T(8,128)(2,1)} %all-gather.8.cloned.1.call-done, bf16[7168,512]{1,0:T(8,128)(2,1)} %all-gather.6.cloned.1.call-done, f32[512,512]{1,0:T(8,128)S(1)} %fusion.33, f32[512,7168]{1,0:T(8,128)} %get-tuple-element.22, f32[7168]{0:T(1024)S(1)} %copy-done.3, ...), kind=kOutput, calls=%fused_computation.9 | convolution fusion | flops 7532445696 | bytes 37779456 | tf_op jit(solution)/shard_map/dot_general | solution.py:110
  387.9 0.0 reduce-scatter.2.cloned.1.call-update
  387.9 80.3 %reduce-scatter.2.cloned.1.call-done = bf16[128,7168]{1,0:T(8,128)(2,1)} async-done(((bf16[512,7168]{1,0:T(8,128)(2,1)}), bf16[128,7168]{1,0:T(8,128)(2,1)}) %reduce-scatter.2.cloned.1.call-update) | async-done | bytes 1835024 | tf_op jit(solution)/shard_map/reduce_scatter | solution.py:109
  468.3 4.2 add_convert_fusion
  472.4 0.0 copy-done.1
  (2 shorter events, 0.0 us)
Async XLA Ops:
  7.4 54.8 %copy-start = (bf16[16,512,128]{2,1,0:T(8,128)(2,1)S(1)}, bf16[16,512,128]{2,1,0:T(8,128)(2,1)}, u32[]{:S(2)}) copy-start(bf16[16,512,128]{2,1,0:T(8,128)(2,1)} %param.17) | copy-start | bytes 6291460
  7.4 335.5 %all-reduce.2.cloned.1.call-start = ((), (), s32[]{:S(2)}) async-start(), calls=%async_computation.1 | async-start | bytes 14680064 | tf_op jit(solution)/shard_map/psum | solution.py:96
  7.4 12.5 %collective-permute-start.3 = (bf16[512,512]{1,0:T(8,128)(2,1)}, bf16[512,512]{1,0:T(8,128)(2,1)}, u32[]{:S(2)}, u32[]{:S(2)}) collective-permute-start(bf16[512,512]{1,0:T(8,128)(2,1)} %param.14), channel_id=1, source_target_pairs={{0,4},{4,8},{8,12},{12,16},{16,20},{20,24},{24,28},{28,0},{1,5},{5... | collective-permute-start | bytes 1572872 | tf_op jit(solution)/shard_map/ppermute | solution.py:20
  7.8 11.8 %collective-permute-start.4 = (bf16[256,128]{1,0:T(8,128)(2,1)}, bf16[256,128]{1,0:T(8,128)(2,1)S(1)}, u32[]{:S(2)}, u32[]{:S(2)}) collective-permute-start(bf16[256,128]{1,0:T(8,128)(2,1)} %param.15), channel_id=1, source_target_pairs={{0,4},{4,8},{8,12},{12,16},{16,20},{20,24},{24,28},{28,0},{1,5},{5... | collective-permute-start | bytes 196616 | tf_op jit(solution)/shard_map/ppermute | solution.py:20
  79.7 24.7 %copy-start.2 = (bf16[128,7168]{1,0:T(8,128)(2,1)S(1)}, bf16[128,7168]{1,0:T(8,128)(2,1)}, u32[]{:S(2)}) copy-start(bf16[128,7168]{1,0:T(8,128)(2,1)} %param.19) | copy-start | bytes 5505028
  103.2 252.4 %all-gather.4.cloned.1.call-start = ((), (), s32[]{:S(2)}) async-start(), calls=%async_computation.2 | async-start | bytes 8257536 | tf_op jit(solution)/shard_map/all_gather | solution.py:102
  103.8 261.6 %all-gather.6.cloned.1.call-start = ((), (), s32[]{:S(2)}) async-start(), calls=%async_computation.3 | async-start | bytes 8257536 | tf_op jit(solution)/shard_map/all_gather | solution.py:103
  104.4 261.0 %all-gather.8.cloned.1.call-start = ((), (), s32[]{:S(2)}) async-start(), calls=%async_computation.4 | async-start | bytes 8257536 | tf_op jit(solution)/shard_map/all_gather | solution.py:104
  104.4 80.0 %collective-permute-start = (bf16[128,7168]{1,0:T(8,128)(2,1)S(1)}, bf16[128,7168]{1,0:T(8,128)(2,1)}, u32[]{:S(2)}, u32[]{:S(2)}) collective-permute-start(bf16[128,7168]{1,0:T(8,128)(2,1)S(1)} %copy-done.2), channel_id=1, source_target_pairs={{0,1},{1,2},{2,3},{3,0},{4,5},{5,6},{6,7},{7,4},{8,9},{9,10},{10,1... | collective-permute-start | bytes 5505032 | tf_op jit(solution)/shard_map/ppermute | solution.py:12
  106.5 361.8 %reduce-scatter.2.cloned.1.call-start = ((), (), s32[]{:S(2)}) async-start(), calls=%async_computation.5 | async-start | bytes 9175040 | tf_op jit(solution)/shard_map/reduce_scatter | solution.py:109
  184.4 60.1 %collective-permute-start.1 = (bf16[128,7168]{1,0:T(8,128)(2,1)}, bf16[128,7168]{1,0:T(8,128)(2,1)}, u32[]{:S(2)}, u32[]{:S(2)}) collective-permute-start(bf16[128,7168]{1,0:T(8,128)(2,1)} %collective-permute-done), channel_id=1, source_target_pairs={{0,1},{1,2},{2,3},{3,0},{4,5},{5,6},{6,7},{7,4},{8,9},{9,10},{10,1... | collective-permute-start | bytes 5505032 | tf_op jit(solution)/shard_map/ppermute | solution.py:12
  244.6 69.2 %collective-permute-start.2 = (bf16[128,7168]{1,0:T(8,128)(2,1)}, bf16[128,7168]{1,0:T(8,128)(2,1)}, u32[]{:S(2)}, u32[]{:S(2)}) collective-permute-start(bf16[128,7168]{1,0:T(8,128)(2,1)} %collective-permute-done.1), channel_id=1, source_target_pairs={{0,1},{1,2},{2,3},{3,0},{4,5},{5,6},{6,7},{7,4},{8,9},{9,10},{10,1... | collective-permute-start | bytes 5505032 | tf_op jit(solution)/shard_map/ppermute | solution.py:12
  334.2 21.4 %copy-start.3 = (f32[7168]{0:T(1024)S(1)}, f32[7168]{0:T(1024)}, u32[]{:S(2)}) copy-start(f32[7168]{0:T(1024)} %param.20) | copy-start | bytes 86020
  365.4 107.1 %copy-start.1 = (bf16[16,512,128]{2,1,0:T(8,128)(2,1)S(1)}, bf16[16,512,128]{2,1,0:T(8,128)(2,1)}, u32[]{:S(2)}) copy-start(bf16[16,512,128]{2,1,0:T(8,128)(2,1)} %param.17) | copy-start | bytes 6291460
Sparse Core Ops, SparseCore 0:
  103.3 239.4 all-reduce.1
  388.0 80.1 reduce-scatter.1
Sparse Core Ops, SparseCore 1:
  105.3 73.2 all-gather.3
  180.0 71.8 all-gather.5
  253.4 71.8 all-gather.7
